TPU v7x, 128 devices: a whole 4x4x4 slice. The times are simulated.
128 devices in a mesh: row: 32 (over y, z, core), col: 4 (over x).
Axes of the slice: x: 4, y: 4, z: 4, core: 2. Of those that a mesh axis runs over, the one named last changes fastest.
Arguments:
- points: bfloat16 [64, 65536], P(None, ('row', 'col')), may hold values from -6 to 6
- lengths: float32 [64], replicated, may hold values from 0.5 to 2
- noise_var: float32 [65536], P(('row', 'col')), may hold values from 0.1 to 1
- solution: float32 [16, 65536], P(None, ('row', 'col')), may hold values from -6 to 6
- residual: float32 [16, 65536], P(None, ('row', 'col')), may hold values from -100 to 100
- direction: float32 [16, 65536], P(None, ('row', 'col')), may hold values from -100 to 100
Outputs:
- new_solution: float32 [16, 65536], P(None, ('row', 'col'))
- new_residual: float32 [16, 65536], P(None, ('row', 'col'))
- new_direction: float32 [16, 65536], P(None, ('row', 'col'))
All inputs are finite; a program needn't handle non-finite values.
Results may differ from a plain program's by a relative error of at most 0.0043.
Values may be sent and summed in bfloat16 or wider, within the bound.
A program may use at most 64 MiB of HBM per device.

v0:
```python
import math

import jax
import jax.numpy as jnp
from jax import lax
from jax.sharding import PartitionSpec as P


def column_squares(scaled):
    values = scaled.astype(jnp.float32)
    return jnp.sum(values * values, axis=0)


def kernel_block(left_cols, left_sq, right_cols, right_sq):
    cross_term = lax.dot_general(
        left_cols, right_cols, (((0,), (0,)), ((), ())), preferred_element_type=jnp.float32
    )
    distance = left_sq[:, None] + right_sq[None, :] - 2.0 * cross_term
    return jnp.exp(-0.5 * distance).astype(jnp.bfloat16)


def grid_image(scaled, narrow_direction):
    row_scaled = lax.all_gather(scaled, "col", axis=1, tiled=True)
    row_sq = column_squares(row_scaled)
    row_count = row_scaled.shape[1]
    zero_start = jnp.zeros((narrow_direction.shape[0], row_count), jnp.float32)
    col_scaled = lax.all_gather(scaled, "row", axis=1, tiled=True)
    col_dir = lax.all_gather(narrow_direction, "row", axis=1, tiled=True)
    col_count = col_scaled.shape[1]
    block_width = math.gcd(col_count, row_count)

    def one_block(block_index, accumulated):
        begin = block_index * block_width
        part_scaled = lax.dynamic_slice_in_dim(col_scaled, begin, block_width, 1)
        part_dir = lax.dynamic_slice_in_dim(col_dir, begin, block_width, 1)
        kernel_tile = kernel_block(part_scaled, column_squares(part_scaled), row_scaled, row_sq)
        return accumulated + jnp.dot(part_dir, kernel_tile, preferred_element_type=jnp.float32)

    partial_value = lax.fori_loop(0, col_count // block_width, one_block, zero_start)
    return lax.psum_scatter(partial_value, "col", scatter_dimension=1, tiled=True)


def local(points, lengths, noise_var, solution, residual, direction):
    scaled = (points.astype(jnp.float32) / lengths[:, None]).astype(jnp.bfloat16)
    narrow_direction = direction.astype(jnp.bfloat16)
    kernel_part = grid_image(scaled, narrow_direction)
    image_field = kernel_part + noise_var[None, :] * direction
    norm_old, curvature = lax.psum(
        (jnp.sum(residual * residual, axis=1), jnp.sum(direction * image_field, axis=1)),
        ("row", "col"),
    )
    step_size = norm_old / curvature
    new_residual = residual - step_size[:, None] * image_field
    norm_new = lax.psum(jnp.sum(new_residual * new_residual, axis=1), ("row", "col"))
    new_solution = solution + step_size[:, None] * direction
    new_direction = new_residual + (norm_new / norm_old)[:, None] * direction
    return (new_solution, new_residual, new_direction)


def solution(mesh):
    placed = (
        P(None, ("row", "col")),
        P(),
        P(("row", "col")),
        P(None, ("row", "col")),
        P(None, ("row", "col")),
        P(None, ("row", "col")),
    )
    return jax.shard_map(
        local,
        mesh=mesh,
        in_specs=placed,
        out_specs=(P(None, ("row", "col")), P(None, ("row", "col")), P(None, ("row", "col"))),
        check_vma=False,
    )
```

profile of v0, /device:TPU:0, one launch (start us, length us, event | category | flops | bytes accessed | tf_op | source)
XLA Modules:
  0.0 267.2 jit_solution(16804422063635153008)
XLA Ops:
  7.2 1.5 divide_convert_fusion
  9.6 12.9 %all_gather.11 = bf16[64,2048]{1,0:T(8,128)(2,1)S(1)} all-gather(bf16[64,512]{1,0:T(8,128)(2,1)} %divide_convert_fusion), channel_id=1, replica_groups=mesh['row'=32,'col'=4] {'col'}, dimensions={1}, use_global_device_ids=true | all-gather | bytes 327680 | tf_op jit(solution)/shard_map/all_gather | solution.py:23
  22.5 26.3 %all_gather.9 = bf16[16,16384]{1,0:T(8,128)(2,1)S(1)} all-gather(bf16[16,512]{1,0:T(8,128)(2,1)S(1)} %convert_element_type.26), channel_id=1, replica_groups=mesh['row'=32,'col'=4] {'row'}, dimensions={1}, use_global_device_ids=true | all-gather | bytes 540672 | tf_op jit(solution)/shard_map/all_gather | solution.py:28
  48.9 8.8 %all-gather.2.cloned.1.call-done = bf16[64,16384]{1,0:T(8,128)(2,1)} async-done(((bf16[64,512]{1,0:T(8,128)(2,1)}), bf16[64,16384]{1,0:T(8,128)(2,1)}) %all-gather.2.cloned.1.call-update) | async-done | bytes 2097168 | tf_op jit(solution)/shard_map/all_gather | solution.py:27
  57.7 51.7 %while.14 = (s32[]{:T(128)}, f32[16,2048]{1,0:T(8,128)S(1)}, bf16[16,16384]{1,0:T(8,128)(2,1)S(1)}, bf16[64,16384]{1,0:T(8,128)(2,1)}, f32[2048]{0:T(1024)S(1)},...) while((s32[]{:T(128)}, f32[16,2048]{1,0:T(8,128)S(1)}, ...), condition=%wide.region_5.0_spmd.clone, body=%wide.region_3.5_spmd.clone.sunk | while | flops 692516864 | bytes 1140384 | solution.py:39
  57.7 1.1 multiply_reduce_fusion.6
  58.8 5.4 %fusion.17 = f32[16,2048]{1,0:T(8,128)S(1)} fusion(bf16[64,2048]{1,0:T(8,128)(2,1)S(1)} %get-tuple-element.213, f32[2048]{0:T(1024)S(1)} %get-tuple-element.212, f32[2048]{0:T(1024)S(1)} %multiply_reduce_fusion.6, bf16[64,16384]{1,0:T(8,128)(2,1)} %get-tuple-element.211, s32[]{:T(128)S(6)} %select_n.10, f32[16,2048]{1,0:T(8,128)S(1)} %get-tuple-element.199, ...), kind=kOutput, calls=%fused_computation.2.clone.1 | convolution fusion | flops 692125696 | bytes 869888 | tf_op jit(solution)/shard_map/while/body/eval_jaxpr/dot_general | solution.py:37
  64.2 1.0 multiply_reduce_fusion.6
  65.2 5.4 %fusion.17 = f32[16,2048]{1,0:T(8,128)S(1)} fusion(bf16[64,2048]{1,0:T(8,128)(2,1)S(1)} %get-tuple-element.213, f32[2048]{0:T(1024)S(1)} %get-tuple-element.212, f32[2048]{0:T(1024)S(1)} %multiply_reduce_fusion.6, bf16[64,16384]{1,0:T(8,128)(2,1)} %get-tuple-element.211, s32[]{:T(128)S(6)} %select_n.10, f32[16,2048]{1,0:T(8,128)S(1)} %get-tuple-element.199, ...), kind=kOutput, calls=%fused_computation.2.clone.1 | convolution fusion | flops 692125696 | bytes 869888 | tf_op jit(solution)/shard_map/while/body/eval_jaxpr/dot_general | solution.py:37
  70.6 1.0 multiply_reduce_fusion.6
  71.7 5.4 %fusion.17 = f32[16,2048]{1,0:T(8,128)S(1)} fusion(bf16[64,2048]{1,0:T(8,128)(2,1)S(1)} %get-tuple-element.213, f32[2048]{0:T(1024)S(1)} %get-tuple-element.212, f32[2048]{0:T(1024)S(1)} %multiply_reduce_fusion.6, bf16[64,16384]{1,0:T(8,128)(2,1)} %get-tuple-element.211, s32[]{:T(128)S(6)} %select_n.10, f32[16,2048]{1,0:T(8,128)S(1)} %get-tuple-element.199, ...), kind=kOutput, calls=%fused_computation.2.clone.1 | convolution fusion | flops 692125696 | bytes 869888 | tf_op jit(solution)/shard_map/while/body/eval_jaxpr/dot_general | solution.py:37
  77.1 1.0 multiply_reduce_fusion.6
  78.1 5.4 %fusion.17 = f32[16,2048]{1,0:T(8,128)S(1)} fusion(bf16[64,2048]{1,0:T(8,128)(2,1)S(1)} %get-tuple-element.213, f32[2048]{0:T(1024)S(1)} %get-tuple-element.212, f32[2048]{0:T(1024)S(1)} %multiply_reduce_fusion.6, bf16[64,16384]{1,0:T(8,128)(2,1)} %get-tuple-element.211, s32[]{:T(128)S(6)} %select_n.10, f32[16,2048]{1,0:T(8,128)S(1)} %get-tuple-element.199, ...), kind=kOutput, calls=%fused_computation.2.clone.1 | convolution fusion | flops 692125696 | bytes 869888 | tf_op jit(solution)/shard_map/while/body/eval_jaxpr/dot_general | solution.py:37
  83.5 1.0 multiply_reduce_fusion.6
  84.6 5.4 %fusion.17 = f32[16,2048]{1,0:T(8,128)S(1)} fusion(bf16[64,2048]{1,0:T(8,128)(2,1)S(1)} %get-tuple-element.213, f32[2048]{0:T(1024)S(1)} %get-tuple-element.212, f32[2048]{0:T(1024)S(1)} %multiply_reduce_fusion.6, bf16[64,16384]{1,0:T(8,128)(2,1)} %get-tuple-element.211, s32[]{:T(128)S(6)} %select_n.10, f32[16,2048]{1,0:T(8,128)S(1)} %get-tuple-element.199, ...), kind=kOutput, calls=%fused_computation.2.clone.1 | convolution fusion | flops 692125696 | bytes 869888 | tf_op jit(solution)/shard_map/while/body/eval_jaxpr/dot_general | solution.py:37
  90.0 1.0 multiply_reduce_fusion.6
  91.0 5.4 %fusion.17 = f32[16,2048]{1,0:T(8,128)S(1)} fusion(bf16[64,2048]{1,0:T(8,128)(2,1)S(1)} %get-tuple-element.213, f32[2048]{0:T(1024)S(1)} %get-tuple-element.212, f32[2048]{0:T(1024)S(1)} %multiply_reduce_fusion.6, bf16[64,16384]{1,0:T(8,128)(2,1)} %get-tuple-element.211, s32[]{:T(128)S(6)} %select_n.10, f32[16,2048]{1,0:T(8,128)S(1)} %get-tuple-element.199, ...), kind=kOutput, calls=%fused_computation.2.clone.1 | convolution fusion | flops 692125696 | bytes 869888 | tf_op jit(solution)/shard_map/while/body/eval_jaxpr/dot_general | solution.py:37
  96.5 1.0 multiply_reduce_fusion.6
  97.5 5.4 %fusion.17 = f32[16,2048]{1,0:T(8,128)S(1)} fusion(bf16[64,2048]{1,0:T(8,128)(2,1)S(1)} %get-tuple-element.213, f32[2048]{0:T(1024)S(1)} %get-tuple-element.212, f32[2048]{0:T(1024)S(1)} %multiply_reduce_fusion.6, bf16[64,16384]{1,0:T(8,128)(2,1)} %get-tuple-element.211, s32[]{:T(128)S(6)} %select_n.10, f32[16,2048]{1,0:T(8,128)S(1)} %get-tuple-element.199, ...), kind=kOutput, calls=%fused_computation.2.clone.1 | convolution fusion | flops 692125696 | bytes 869888 | tf_op jit(solution)/shard_map/while/body/eval_jaxpr/dot_general | solution.py:37
  104.0 5.4 %fusion.17 = f32[16,2048]{1,0:T(8,128)S(1)} fusion(bf16[64,2048]{1,0:T(8,128)(2,1)S(1)} %get-tuple-element.213, f32[2048]{0:T(1024)S(1)} %get-tuple-element.212, f32[2048]{0:T(1024)S(1)} %multiply_reduce_fusion.6, bf16[64,16384]{1,0:T(8,128)(2,1)} %get-tuple-element.211, s32[]{:T(128)S(6)} %select_n.10, f32[16,2048]{1,0:T(8,128)S(1)} %get-tuple-element.199, ...), kind=kOutput, calls=%fused_computation.2.clone.1 | convolution fusion | flops 692125696 | bytes 869888 | tf_op jit(solution)/shard_map/while/body/eval_jaxpr/dot_general | solution.py:37
  110.2 19.8 %reduce-scatter.2.cloned.1.call-done = f32[16,512]{1,0:T(8,128)} async-done(((f32[16,2048]{1,0:T(8,128)}), f32[16,512]{1,0:T(8,128)}) %reduce-scatter.2.cloned.1.call-update) | async-done | bytes 32784 | tf_op jit(solution)/shard_map/reduce_scatter | solution.py:40
  130.9 65.2 %all-reduce = (f32[16]{0:T(128)S(1)}, f32[16]{0:T(128)S(1)}) all-reduce(f32[16]{0:T(128)S(1)} %multiply_reduce_fusion.4, f32[16]{0:T(128)S(1)} %multiply_reduce_fusion.3), channel_id=1, replica_groups=mesh['row'=32,'col'=4] {'row','col'}, use_global_device_ids=true, to_apply=%region_1.2 | all-reduce | flops 32 | bytes 256 | tf_op jit(solution)/shard_map/psum | solution.py:48
  196.1 1.6 multiply_reduce_fusion.2
  197.7 62.0 %psum.23 = f32[16]{0:T(128)S(1)} all-reduce(f32[16]{0:T(128)S(1)} %get-tuple-element.148), channel_id=1, replica_groups=mesh['row'=32,'col'=4] {'row','col'}, use_global_device_ids=true, to_apply=%region_10.0 | all-reduce | flops 16 | bytes 128 | tf_op jit(solution)/shard_map/psum | solution.py:54
  (25 shorter events, 4.3 us)
Async XLA Ops:
  7.2 50.5 %all-gather.2.cloned.1.call-start = ((), (), s32[]{:S(2)}) async-start(), calls=%async_computation.1 | async-start | bytes 2162688 | tf_op jit(solution)/shard_map/all_gather | solution.py:27
  8.8 121.2 %reduce-scatter.2.cloned.1.call-start = ((), (), s32[]{:S(2)}) async-start(), calls=%async_computation.2 | async-start | bytes 163840 | tf_op jit(solution)/shard_map/reduce_scatter | solution.py:40
  57.7 52.4 %copy-start.2 = (f32[16,512]{1,0:T(8,128)S(1)}, f32[16,512]{1,0:T(8,128)}, u32[]{:S(2)}) copy-start(f32[16,512]{1,0:T(8,128)} %param.12) | copy-start | bytes 98308
  57.7 72.3 %copy-start = (f32[16,512]{1,0:T(8,128)S(1)}, f32[16,512]{1,0:T(8,128)}, u32[]{:S(2)}) copy-start(f32[16,512]{1,0:T(8,128)} %param.13) | copy-start | bytes 98308
  57.7 72.3 %copy-start.5 = (f32[512]{0:T(512)S(1)}, f32[512]{0:T(512)}, u32[]{:S(2)}) copy-start(f32[512]{0:T(512)} %param.10) | copy-start | bytes 6148
  57.7 138.4 %copy-start.4 = (f32[16,512]{1,0:T(8,128)S(1)}, f32[16,512]{1,0:T(8,128)}, u32[]{:S(2)}) copy-start(f32[16,512]{1,0:T(8,128)} %param.11) | copy-start | bytes 98308
  109.4 0.7 copy-start.3
  197.7 62.7 %copy-start.1 = (f32[16,512]{1,0:T(8,128)}, f32[16,512]{1,0:T(8,128)S(1)}, u32[]{:S(2)}) copy-start(f32[16,512]{1,0:T(8,128)S(1)} %get-tuple-element.149) | copy-start | bytes 98308
Sparse Core Ops, SparseCore 0:
  10.2 47.4 all-gather.1
  110.2 19.7 reduce-scatter.1
where the time goes:
time: 269 us; the launch traced here: 267 us
  blocking collectives  166 us (62%)
  matrix products  43.3 us (16%)
  waiting for transfers between devices  28.7 us (11%)
  between operations  14.1 us (5%)
  other arithmetic  13.9 us (5%)
    psum x1, blocking collectives, local(): lax.psum((jnp.sum(residual * residual, axis=1), jnp.sum(direction * image...  65.2 us
    psum x1, blocking collectives, local(): lax.psum(jnp.sum(new_residual * new_residual, axis=1), ('row', 'col'))  62 us
    dot_general x8, matrix products, one_block(): jnp.dot(part_dir, kernel_tile, preferred_element_type=jnp.float32)  43.3 us
    all_gather x1, blocking collectives, grid_image(): col_dir = lax.all_gather(narrow_direction, 'row', axis=1, tiled=True)  26.3 us
    reduce_scatter x1, waiting for transfers between devices, grid_image(): lax.psum_scatter(partial_value, 'col', scatter_dimension=1, tiled=True)  19.8 us
    all_gather x1, blocking collectives, grid_image(): row_scaled = lax.all_gather(scaled, 'col', axis=1, tiled=True)  12.9 us
    all_gather x1, waiting for transfers between devices, grid_image(): col_scaled = lax.all_gather(scaled, 'row', axis=1, tiled=True)  8.81 us
    reduce_sum x9, other arithmetic, column_squares(): return jnp.sum(values * values, axis=0)  8.36 us
  transfers between devices with their start and end apart: 2, of which 2 were waited for; matrix products, arithmetic and copies ran while one was open for 0% of the time, Pallas kernels for 0%

commit v1 on v0

v1 whole, which is shorter than its diff:
```python
import functools

import jax
import jax.numpy as jnp
from jax import lax
from jax.experimental import pallas as pl
from jax.experimental.pallas import tpu as pltpu
from jax.sharding import PartitionSpec as P

MESH = pl.DeviceIdType.MESH
FEAT = 64
RHS = 16
DEEP = FEAT + 16
ROWS = DEEP + RHS
SIDE = 4


def plane_order():
    hops = lambda d: min(d, SIDE - d)
    pairs = [(a, b) for a in range(SIDE) for b in range(SIDE)]
    return sorted(pairs, key=lambda p: (hops(p[0]) + hops(p[1]), p))


def bias_rows(scaled, flip):
    values = scaled.astype(jnp.float32)
    half = -0.5 * jnp.sum(values * values, axis=0, keepdims=True)
    high = half.astype(jnp.bfloat16).astype(jnp.float32)
    rest = half - high
    middle = rest.astype(jnp.bfloat16).astype(jnp.float32)
    low = rest - middle
    width = scaled.shape[1]
    index = lax.broadcasted_iota(jnp.int32, (16, width), 0)
    first = 3 if flip else 0
    ones = 0 if flip else 3
    rows = jnp.where(index == first, high, 0.0)
    rows = jnp.where(index == first + 1, middle, rows)
    rows = jnp.where(index == first + 2, low, rows)
    rows = jnp.where((index >= ones) & (index < ones + 3), 1.0, rows)
    return rows.astype(jnp.bfloat16)


def kernel(
    points_ref, lengths_ref, noise_ref, solution_ref, residual_ref, direction_ref,
    new_solution_ref, new_residual_ref, new_direction_ref,
    blocks, line, weights, total, parts, sums_line, sums_plane, own_sums, line_sums,
    plane_send, plane_recv, pair_send, pair_recv, line_send, line_recv,
    part_send, part_recv, sl_send, sl_recv, sp_send, sp_recv,
):
    width = points_ref.shape[1]
    row, col = lax.axis_index("row"), lax.axis_index("col")
    core = lax.rem(row, 2)
    chip = row // 2
    y, z = chip // SIDE, lax.rem(chip, SIDE)
    order = plane_order()

    def at(dy, dz, dcore, dx):
        ny, nz = lax.rem(y + dy, SIDE), lax.rem(z + dz, SIDE)
        ncore = lax.rem(core + dcore, 2)
        return ((ny * SIDE + nz) * 2 + ncore, lax.rem(col + dx, SIDE))

    plane = [at(dy, dz, 0, 0) for dy, dz in order[1:]]
    others = [(q, c) for c in range(2) for q in range(SIDE)][1:]
    row_line = [at(0, 0, c, q) for q, c in others]
    sibling = at(0, 0, 1, 0)

    barrier = pltpu.get_barrier_semaphore()
    for device in plane + row_line:
        pl.semaphore_signal(barrier, inc=1, device_id=device, device_id_type=MESH)

    diagonal = lax.broadcasted_iota(jnp.int32, (FEAT, FEAT), 0) == lax.broadcasted_iota(
        jnp.int32, (FEAT, FEAT), 1
    )
    lengths = jnp.sum(jnp.where(diagonal, lengths_ref[...], 0.0), axis=1, keepdims=True)
    scaled = (points_ref[...].astype(jnp.float32) / lengths).astype(jnp.bfloat16)
    blocks[0, 0:FEAT, :] = scaled
    blocks[0, FEAT:DEEP, :] = bias_rows(scaled, False)
    blocks[0, DEEP:ROWS, :] = direction_ref[...].astype(jnp.bfloat16)

    pl.semaphore_wait(barrier, len(plane) + len(row_line))

    def remote(src, dst, send, recv, device):
        return pltpu.make_async_remote_copy(
            src_ref=src, dst_ref=dst, send_sem=send, recv_sem=recv, device_id=device, device_id_type=MESH
        )

    line_copies = [
        remote(blocks.at[0, pl.ds(0, FEAT)], line.at[q - 1], line_send.at[q - 1], line_recv.at[q - 1], at(0, 0, 0, q))
        for q in range(1, SIDE)
    ]
    for copy in line_copies:
        copy.start()
    plane_copies = [
        remote(blocks.at[0], blocks.at[k + 1], plane_send.at[k], plane_recv.at[k], plane[k]) for k in range(len(plane))
    ]
    for copy in plane_copies:
        copy.start()

    def pair_copy(p):
        return remote(blocks.at[p], blocks.at[16 + p], pair_send.at[p], pair_recv.at[p], sibling)

    weights[0:FEAT, 0:width] = scaled
    weights[FEAT:DEEP, 0:width] = bias_rows(scaled, True)
    for q in range(1, SIDE):
        line_copies[q - 1].wait_recv()
        part = line[q - 1]
        weights[0:FEAT, q * width : (q + 1) * width] = part
        weights[FEAT:DEEP, q * width : (q + 1) * width] = bias_rows(part, True)

    total[...] = jnp.zeros_like(total)

    def work(k):
        cross = lax.dot_general(
            blocks[k, 0:DEEP, :], weights[...], (((0,), (0,)), ((), ())), preferred_element_type=jnp.float32
        )
        tile = jnp.exp(cross).astype(jnp.bfloat16)
        total[...] += jnp.dot(blocks[k, DEEP:ROWS, :], tile, preferred_element_type=jnp.float32)

    pair_copy(0).start()
    work(0)
    pair_copy(0).wait_recv()
    work(16)

    def step(p, carry):
        remote(
            blocks.at[0], blocks.at[p], plane_send.at[p - 1], plane_recv.at[p - 1], plane[0]
        ).wait_recv()
        pair_copy(p).start()
        work(p)
        pair_copy(p).wait_recv()
        work(16 + p)
        return carry

    lax.fori_loop(1, 16, step, 0)

    part_copies = [
        remote(
            total.at[:, pl.ds(q * width, width)], parts.at[q - 1], part_send.at[q - 1], part_recv.at[q - 1],
            at(0, 0, 0, SIDE - q),
        )
        for q in range(1, SIDE)
    ]
    for copy in part_copies:
        copy.start()
    residual, direction = residual_ref[...], direction_ref[...]
    image = total[:, 0:width] + noise_ref[...] * direction
    for q in range(1, SIDE):
        part_copies[q - 1].wait_recv()
        image = image + parts[q - 1]

    lane = lax.broadcasted_iota(jnp.int32, (RHS, 128), 1)
    packed = jnp.zeros((RHS, 128), jnp.float32)
    for n, product in enumerate((residual * residual, direction * image, residual * image, image * image)):
        packed = jnp.where(lane == n, jnp.sum(product, axis=1, keepdims=True), packed)
    own_sums[...] = packed
    sl_copies = [
        remote(own_sums, sums_line.at[n], sl_send.at[n], sl_recv.at[n], row_line[n]) for n in range(len(row_line))
    ]
    for copy in sl_copies:
        copy.start()
    for n, copy in enumerate(sl_copies):
        copy.wait_recv()
        packed = packed + sums_line[n]
    line_sums[...] = packed
    sp_copies = [
        remote(line_sums, sums_plane.at[n], sp_send.at[n], sp_recv.at[n], plane[n]) for n in range(len(plane))
    ]
    for copy in sp_copies:
        copy.start()
    for n, copy in enumerate(sp_copies):
        copy.wait_recv()
        packed = packed + sums_plane[n]

    norm_old, curvature, mixed, square = (packed[:, n : n + 1] for n in range(4))
    step_size = norm_old / curvature
    norm_new = norm_old + step_size * (step_size * square - 2.0 * mixed)
    new_residual = residual - step_size * image
    new_solution_ref[...] = solution_ref[...] + step_size * direction
    new_residual_ref[...] = new_residual
    new_direction_ref[...] = new_residual + (norm_new / norm_old) * direction

    for copy in line_copies + plane_copies + part_copies + sl_copies + sp_copies:
        copy.wait_send()
    for p in range(16):
        pair_copy(p).wait_send()


def local(points, lengths, noise_var, solution, residual, direction):
    width = points.shape[1]
    out = jax.ShapeDtypeStruct((RHS, width), jnp.float32)
    vmem = pl.BlockSpec(memory_space=pltpu.VMEM)
    dma = pltpu.SemaphoreType.DMA
    return pl.pallas_call(
        kernel,
        out_shape=(out, out, out),
        in_specs=[vmem] * 6,
        out_specs=(vmem,) * 3,
        scratch_shapes=[
            pltpu.VMEM((32, ROWS, width), jnp.bfloat16),
            pltpu.VMEM((SIDE - 1, FEAT, width), jnp.bfloat16),
            pltpu.VMEM((DEEP, SIDE * width), jnp.bfloat16),
            pltpu.VMEM((RHS, SIDE * width), jnp.float32),
            pltpu.VMEM((SIDE - 1, RHS, width), jnp.float32),
            pltpu.VMEM((7, RHS, 128), jnp.float32),
            pltpu.VMEM((15, RHS, 128), jnp.float32),
            pltpu.VMEM((RHS, 128), jnp.float32),
            pltpu.VMEM((RHS, 128), jnp.float32),
            dma((15,)), dma((15,)), dma((16,)), dma((16,)), dma((3,)), dma((3,)),
            dma((3,)), dma((3,)), dma((7,)), dma((7,)), dma((15,)), dma((15,)),
        ],
        compiler_params=pltpu.CompilerParams(
            collective_id=0, has_side_effects=True, vmem_limit_bytes=48 << 20
        ),
        name="cg_step",
    )(points, lengths.reshape(1, FEAT), noise_var.reshape(1, width), solution, residual, direction)


def solution(mesh):
    wide = P(None, ("row", "col"))
    return jax.shard_map(
        local,
        mesh=mesh,
        in_specs=(wide, P(), P(("row", "col")), wide, wide, wide),
        out_specs=(wide, wide, wide),
        check_vma=False,
    )
```

time: 269 us -> 71.6 us (0.27)
  blocking collectives: 166 us -> 0 us
  Pallas kernels: 0 us -> 64.6 us
  matrix products: 43.3 us -> 0 us
  waiting for transfers between devices: 28.7 us -> 0 us
  other arithmetic: 13.9 us -> 0 us
  between operations: 14.1 us -> 0.66 us
  local copies, waits for them, and re-layouts: 0.67 us -> 5.63 us
    psum x2 -> x0, blocking collectives: 127 us -> none  [the longest x1 65.2 us: local(): lax.psum((jnp.sum(residual * residual, axis=1), jnp.sum(direction * image...]
    pallas_call x0 -> x1, Pallas kernels: none -> 64.6 us  [local(): pl.pallas_call(kernel, out_shape=(out, out, out), in_specs=[vmem] * 6, ou...]
    dot_general x8 -> x0, matrix products: 43.3 us -> none  [one_block(): jnp.dot(part_dir, kernel_tile, preferred_element_type=jnp.float32)]
    all_gather x2 -> x0, blocking collectives: 39.2 us -> none  [the longest x1 26.3 us: grid_image(): col_dir = lax.all_gather(narrow_direction, 'row', axis=1, tiled=True)]
    reduce_scatter x1 -> x0, waiting for transfers between devices: 19.8 us -> none  [grid_image(): lax.psum_scatter(partial_value, 'col', scatter_dimension=1, tiled=True)]
    reduce_sum x12 -> x0, other arithmetic: 10.9 us -> none  [the longest x9 8.36 us: column_squares(): return jnp.sum(values * values, axis=0)]
    all_gather x1 -> x0, waiting for transfers between devices: 8.81 us -> none  [grid_image(): col_scaled = lax.all_gather(scaled, 'row', axis=1, tiled=True)]
    unnamed x12 -> x15, local copies, waits for them, and re-layouts: 0.67 us -> 5.63 us
  transfers between devices with their start and end apart: 2 -> 0, of which waited for: 2 -> 0; matrix products, arithmetic and copies ran while one was open for 0% -> 0% of each run, Pallas kernels for 0% -> 0%
where the time goes in v1:
time: 71.6 us; the launch traced here: 70.9 us
  Pallas kernels  64.6 us (90%)
  local copies, waits for them, and re-layouts  5.63 us (8%)
    pallas_call x1, Pallas kernels, local(): pl.pallas_call(kernel, out_shape=(out, out, out), in_specs=[vmem] * 6, ou...  64.6 us
    unnamed x15, local copies, waits for them, and re-layouts  5.63 us

profile of v1, /device:TPU:0, one launch (start us, length us, event | category | flops | bytes accessed | tf_op | source)
XLA Modules:
  0.0 70.9 jit_solution(12130744313803952004)
XLA Ops:
  0.6 0.0 copy-start.4
  0.6 0.0 copy-start.5
  0.7 0.7 copy-done.4
  1.3 0.0 copy-done.5
  1.3 0.0 copy-start
  1.3 0.8 %copy-done = bf16[64,512]{1,0:T(8,128)(2,1)S(1)} copy-done((bf16[64,512]{1,0:T(8,128)(2,1)S(1)}, bf16[64,512]{1,0:T(8,128)(2,1)}, u32[]{:S(2)}) %copy-start) | copy-done | bytes 65560
  2.2 0.0 copy-start.1
  2.2 0.8 %copy-done.1 = f32[16,512]{1,0:T(8,128)S(1)} copy-done((f32[16,512]{1,0:T(8,128)S(1)}, f32[16,512]{1,0:T(8,128)}, u32[]{:S(2)}) %copy-start.1) | copy-done | bytes 32792
  2.9 0.0 copy-start.2
  2.9 0.8 %copy-done.2 = f32[16,512]{1,0:T(8,128)S(1)} copy-done((f32[16,512]{1,0:T(8,128)S(1)}, f32[16,512]{1,0:T(8,128)}, u32[]{:S(2)}) %copy-start.2) | copy-done | bytes 32792
  3.7 0.0 copy-start.3
  3.7 0.8 %copy-done.3 = f32[16,512]{1,0:T(8,128)S(1)} copy-done((f32[16,512]{1,0:T(8,128)S(1)}, f32[16,512]{1,0:T(8,128)}, u32[]{:S(2)}) %copy-start.3) | copy-done | bytes 32792
  4.4 64.6 %cg_step.1 = (f32[16,512]{1,0:T(8,128)S(1)}, f32[16,512]{1,0:T(8,128)S(1)}, f32[16,512]{1,0:T(8,128)S(1)}) custom-call(bf16[64,512]{1,0:T(8,128)(2,1)S(1)} %copy-done, f32[1,64]{1,0:T(1,128)S(1)} %bitcast.3, f32[1,512]{1,0:T(1,128)S(1)} %bitcast.2, f32[16,512]{1,0:T(8,128)S(1)} %copy-done.1, f32[16,512]{1,0:T(8,128)S(1)} %copy-done.2, f32[16,512]{1,0:T(8,128)S(1)} %copy-done.3), custom_call_target="tpu_custom_call" | custom-call | tf_op jit(solution)/shard_map/cg_step/pallas_call | solution.py:192
  69.0 0.6 copy.12
  69.7 0.6 copy.13
  70.3 0.6 copy.14
Async XLA Ops:
  0.6 0.7 copy-start.4
  0.6 0.7 copy-start.5
  1.3 0.8 %copy-start = (bf16[64,512]{1,0:T(8,128)(2,1)S(1)}, bf16[64,512]{1,0:T(8,128)(2,1)}, u32[]{:S(2)}) copy-start(bf16[64,512]{1,0:T(8,128)(2,1)} %points_ref.1) | copy-start | bytes 196612
  2.2 0.8 %copy-start.1 = (f32[16,512]{1,0:T(8,128)S(1)}, f32[16,512]{1,0:T(8,128)}, u32[]{:S(2)}) copy-start(f32[16,512]{1,0:T(8,128)} %solution_ref.1) | copy-start | bytes 98308
  2.9 0.8 %copy-start.2 = (f32[16,512]{1,0:T(8,128)S(1)}, f32[16,512]{1,0:T(8,128)}, u32[]{:S(2)}) copy-start(f32[16,512]{1,0:T(8,128)} %residual_ref.1) | copy-start | bytes 98308
  3.7 0.8 %copy-start.3 = (f32[16,512]{1,0:T(8,128)S(1)}, f32[16,512]{1,0:T(8,128)}, u32[]{:S(2)}) copy-start(f32[16,512]{1,0:T(8,128)} %direction_ref.1) | copy-start | bytes 98308

commit v2 on v1

v2 whole, which is shorter than its diff:
```python
import functools

import jax
import jax.numpy as jnp
from jax import lax
from jax.experimental import pallas as pl
from jax.experimental.pallas import tpu as pltpu
from jax.sharding import PartitionSpec as P

MESH = pl.DeviceIdType.MESH
FEAT = 64
RHS = 16
DEEP = FEAT + 16
ROWS = DEEP + RHS
SIDE = 4
LATE = 11


def plane_order():
    near = (0, 1, 3, 2)
    first = [(a, 0) for a in near] + [(0, b) for b in near[1:]]
    return first + [(a, b) for b in near[1:] for a in near[1:]]


def bias_rows(scaled, flip):
    values = scaled.astype(jnp.float32)
    half = -0.5 * jnp.sum(values * values, axis=0, keepdims=True)
    high = half.astype(jnp.bfloat16).astype(jnp.float32)
    rest = half - high
    middle = rest.astype(jnp.bfloat16).astype(jnp.float32)
    low = rest - middle
    width = scaled.shape[1]
    index = lax.broadcasted_iota(jnp.int32, (16, width), 0)
    first = 3 if flip else 0
    ones = 0 if flip else 3
    rows = jnp.where(index == first, high, 0.0)
    rows = jnp.where(index == first + 1, middle, rows)
    rows = jnp.where(index == first + 2, low, rows)
    rows = jnp.where((index >= ones) & (index < ones + 3), 1.0, rows)
    return rows.astype(jnp.bfloat16)


def kernel(
    points_hbm, lengths_hbm, noise_hbm, solution_hbm, residual_hbm, direction_hbm,
    new_solution_ref, new_residual_ref, new_direction_ref,
    points_ref, lengths_ref, noise_ref, solution_ref, residual_ref, direction_ref,
    blocks, line, weights, lefts, cross, tiles, total, parts, sums_line, sums_plane, own_sums, line_sums,
    in_sem, plane_send, plane_recv, pair_send, pair_recv, line_send, line_recv,
    part_send, part_recv, sl_send, sl_recv, sp_send, sp_recv,
):
    width = points_ref.shape[1]
    row, col = lax.axis_index("row"), lax.axis_index("col")
    core = lax.rem(row, 2)
    chip = row // 2
    y, z = chip // SIDE, lax.rem(chip, SIDE)
    order = plane_order()
    slot_of = {offset: n for n, offset in enumerate(order)}

    def at(first, second, dcore, dx):
        dy = first * core + second * (1 - core)
        dz = first * (1 - core) + second * core
        ny, nz = lax.rem(y + dy, SIDE), lax.rem(z + dz, SIDE)
        return ((ny * SIDE + nz) * 2 + lax.rem(core + dcore, 2), lax.rem(col + dx, SIDE))

    plane = [at(a, b, 0, 0) for a, b in order[1:]]
    others = [(q, c) for c in range(2) for q in range(SIDE)][1:]
    row_line = [at(0, 0, c, q) for q, c in others]
    sibling = at(0, 0, 1, 0)

    barrier = pltpu.get_barrier_semaphore()
    greeted = plane[:6] + row_line
    for device in greeted:
        pl.semaphore_signal(barrier, inc=1, device_id=device, device_id_type=MESH)

    pairs = (
        (points_hbm, points_ref), (lengths_hbm, lengths_ref), (direction_hbm, direction_ref),
        (noise_hbm, noise_ref), (solution_hbm, solution_ref), (residual_hbm, residual_ref),
    )
    loads = [pltpu.make_async_copy(src, dst, in_sem.at[n]) for n, (src, dst) in enumerate(pairs)]
    for copy in loads:
        copy.start()
    total[...] = jnp.zeros_like(total)
    cross[1] = jnp.full(cross.shape[1:], -1e4, jnp.float32)
    tiles[0] = jnp.zeros(tiles.shape[1:], jnp.bfloat16)
    for copy in loads[:3]:
        copy.wait()

    diagonal = lax.broadcasted_iota(jnp.int32, (FEAT, FEAT), 0) == lax.broadcasted_iota(
        jnp.int32, (FEAT, FEAT), 1
    )
    lengths = jnp.sum(jnp.where(diagonal, lengths_ref[...], 0.0), axis=1, keepdims=True)
    scaled = (points_ref[...].astype(jnp.float32) / lengths).astype(jnp.bfloat16)
    blocks[0, 0:FEAT, :] = scaled
    blocks[0, FEAT:DEEP, :] = bias_rows(scaled, False)
    blocks[0, DEEP:ROWS, :] = direction_ref[...].astype(jnp.bfloat16)

    pl.semaphore_wait(barrier, len(greeted))

    def remote(src, dst, send, recv, device):
        return pltpu.make_async_remote_copy(
            src_ref=src, dst_ref=dst, send_sem=send, recv_sem=recv, device_id=device, device_id_type=MESH
        )

    def plane_copy(src, dst, device):
        return remote(blocks.at[src], blocks.at[dst], plane_send.at[dst - 1], plane_recv.at[dst - 1], device)

    def pair_copy(p):
        return remote(blocks.at[p], blocks.at[16 + p], pair_send.at[p], pair_recv.at[p], sibling)

    line_copies = [
        remote(blocks.at[0, pl.ds(0, FEAT)], line.at[q - 1], line_send.at[q - 1], line_recv.at[q - 1], at(0, 0, 0, q))
        for q in (1, 3, 2)
    ]
    plane_copies = [plane_copy(0, k, plane[k - 1]) for k in range(1, 7)]
    pair_copy(0).start()
    for copy in line_copies[:2] + plane_copies[:2] + line_copies[2:] + plane_copies[2:]:
        copy.start()

    def transpose(block):
        lefts[block, :, 0:DEEP] = blocks[block, 0:DEEP, :].T

    weights[0:FEAT, 0:width] = scaled
    weights[FEAT:DEEP, 0:width] = bias_rows(scaled, True)
    transpose(0)
    for copy, q in zip(line_copies, (1, 3, 2)):
        copy.wait_recv()
        part = line[q - 1]
        weights[0:FEAT, q * width : (q + 1) * width] = part
        weights[FEAT:DEEP, q * width : (q + 1) * width] = bias_rows(part, True)

    for k in range(1, 4):
        plane_copies[k - 1].wait_recv()
        first = order[k][0]
        for second in (1, 3, 2):
            copy = plane_copy(k, slot_of[first, second], at(0, second, 0, 0))
            copy.start()
            plane_copies.append(copy)

    def cross_stage(block, q, slot):
        cross[slot] = jnp.dot(
            lefts[block, :, 0:DEEP], weights[:, q * width : (q + 1) * width], preferred_element_type=jnp.float32
        )

    def exp_stage(slot):
        tiles[slot] = jnp.exp(cross[slot]).astype(jnp.bfloat16)

    def sum_stage(block, q, slot):
        total[:, q * width : (q + 1) * width] += jnp.dot(
            blocks[block, DEEP:ROWS, :], tiles[slot], preferred_element_type=jnp.float32
        )

    def body(parts_done, p, carry):
        before = jnp.maximum(p - 1, 0)
        after = jnp.minimum(p + 1, 15)

        @pl.when((p < 15) & (p > 2))
        def _():
            remote(
                blocks.at[0], blocks.at[after], plane_send.at[after - 1], plane_recv.at[after - 1], plane[0]
            ).wait_recv()

        @pl.when(p < 15)
        def _():
            pair_copy(after).start()

        pair_copy(p).wait_recv()
        transpose(16 + p)
        chunks = [(16 * half + p, q) for half in range(2) for q in range(SIDE) if q or not parts_done]
        lagged = [(16 + before, 2), (16 + before, 3)] + chunks
        for c, (block, q) in enumerate(chunks):
            sum_stage(*lagged[c], c % 2)
            exp_stage((c + 1) % 2)
            cross_stage(block, q, c % 2)
            if c == len(chunks) // 2 - 1:
                transpose(after)
        return carry

    lax.fori_loop(0, 16 - LATE, functools.partial(body, False), 0)
    lax.fori_loop(16 - LATE, 16, functools.partial(body, True), 0)

    def late(n):
        return 16 * lax.rem(n, 2) + 16 - LATE + n // 2

    sum_stage(31, 2, 0)
    exp_stage(1)
    cross_stage(late(0), 0, 0)
    sum_stage(31, 3, 1)
    exp_stage(0)
    cross_stage(late(1), 0, 1)
    part_copies = [
        remote(
            total.at[:, pl.ds(q * width, width)], parts.at[q - 1], part_send.at[q - 1], part_recv.at[q - 1],
            at(0, 0, 0, SIDE - q),
        )
        for q in (1, 3, 2)
    ]
    for copy in part_copies:
        copy.start()

    def own(m, carry):
        for c in range(6):
            n = 6 * m + 2 + c
            sum_stage(late(n - 2), 0, c % 2)
            exp_stage((c + 1) % 2)
            cross_stage(late(n), 0, c % 2)
        return carry

    lax.fori_loop(0, (2 * LATE - 4) // 6, own, 0)
    for n in (2 * LATE - 2, 2 * LATE - 1):
        sum_stage(late(n - 2), 0, n % 2)
        exp_stage((n + 1) % 2)
        cross_stage(late(n), 0, n % 2)
    sum_stage(late(2 * LATE - 2), 0, 0)
    exp_stage(1)
    sum_stage(late(2 * LATE - 1), 0, 1)
    for copy in loads[3:]:
        copy.wait()
    residual, direction = residual_ref[...], direction_ref[...]
    image = total[:, 0:width] + noise_ref[...] * direction
    for copy, q in zip(part_copies, (1, 3, 2)):
        copy.wait_recv()
        image = image + parts[q - 1]

    lane = lax.broadcasted_iota(jnp.int32, (RHS, 128), 1)
    packed = jnp.zeros((RHS, 128), jnp.float32)
    for n, product in enumerate((residual * residual, direction * image, residual * image, image * image)):
        packed = jnp.where(lane == n, jnp.sum(product, axis=1, keepdims=True), packed)
    own_sums[...] = packed
    sl_copies = [
        remote(own_sums, sums_line.at[n], sl_send.at[n], sl_recv.at[n], row_line[n]) for n in range(len(row_line))
    ]
    for copy in sl_copies:
        copy.start()
    for n, copy in enumerate(sl_copies):
        copy.wait_recv()
        packed = packed + sums_line[n]
    line_sums[...] = packed
    sp_copies = [
        remote(line_sums, sums_plane.at[n], sp_send.at[n], sp_recv.at[n], plane[n]) for n in range(len(plane))
    ]
    for copy in sp_copies:
        copy.start()
    for n, copy in enumerate(sp_copies):
        copy.wait_recv()
        packed = packed + sums_plane[n]

    norm_old, curvature, mixed, square = (packed[:, n : n + 1] for n in range(4))
    step_size = norm_old / curvature
    norm_new = norm_old + step_size * (step_size * square - 2.0 * mixed)
    new_residual = residual - step_size * image
    new_solution_ref[...] = solution_ref[...] + step_size * direction
    new_residual_ref[...] = new_residual
    new_direction_ref[...] = new_residual + (norm_new / norm_old) * direction

    for copy in line_copies + plane_copies + part_copies + sl_copies + sp_copies:
        copy.wait_send()
    for p in range(16):
        pair_copy(p).wait_send()


def local(points, lengths, noise_var, solution, residual, direction):
    width = points.shape[1]
    out = jax.ShapeDtypeStruct((RHS, width), jnp.float32)
    vmem, dma = pltpu.VMEM, pltpu.SemaphoreType.DMA
    wide = vmem((RHS, width), jnp.float32)
    return pl.pallas_call(
        kernel,
        out_shape=(out, out, out),
        in_specs=[pl.BlockSpec(memory_space=pl.ANY)] * 6,
        out_specs=(pl.BlockSpec(memory_space=vmem),) * 3,
        scratch_shapes=[
            vmem((FEAT, width), jnp.bfloat16),
            vmem((1, FEAT), jnp.float32),
            vmem((1, width), jnp.float32),
            wide,
            wide,
            wide,
            vmem((32, ROWS, width), jnp.bfloat16),
            vmem((SIDE - 1, FEAT, width), jnp.bfloat16),
            vmem((DEEP, SIDE * width), jnp.bfloat16),
            vmem((32, width, 128), jnp.bfloat16),
            vmem((2, width, width), jnp.float32),
            vmem((2, width, width), jnp.bfloat16),
            vmem((RHS, SIDE * width), jnp.float32),
            vmem((SIDE - 1, RHS, width), jnp.float32),
            vmem((7, RHS, 128), jnp.float32),
            vmem((15, RHS, 128), jnp.float32),
            vmem((RHS, 128), jnp.float32),
            vmem((RHS, 128), jnp.float32),
            dma((6,)), dma((15,)), dma((15,)), dma((16,)), dma((16,)), dma((3,)), dma((3,)),
            dma((3,)), dma((3,)), dma((7,)), dma((7,)), dma((15,)), dma((15,)),
        ],
        compiler_params=pltpu.CompilerParams(
            collective_id=0, has_side_effects=True, vmem_limit_bytes=63 << 20
        ),
        name="cg_step",
    )(points, lengths.reshape(1, FEAT), noise_var.reshape(1, width), solution, residual, direction)


def solution(mesh):
    wide = P(None, ("row", "col"))
    return jax.shard_map(
        local,
        mesh=mesh,
        in_specs=(wide, P(), P(("row", "col")), wide, wide, wide),
        out_specs=(wide, wide, wide),
        check_vma=False,
    )
```

time: 71.6 us -> 57.8 us (0.81)
  Pallas kernels: 64.6 us -> 53.9 us
  local copies, waits for them, and re-layouts: 5.63 us -> 2.77 us
    pallas_call x1, Pallas kernels: 64.6 us -> 53.9 us  [local(): pl.pallas_call(kernel, out_shape=(out, out, out), in_specs=[pl.BlockSpec(...]
    unnamed x15 -> x7, local copies, waits for them, and re-layouts: 5.63 us -> 2.77 us
where the time goes in v2:
time: 57.8 us; the launch traced here: 57.3 us
  Pallas kernels  53.9 us (93%)
  local copies, waits for them, and re-layouts  2.77 us (5%)
  between operations  0.65 us (1%)
    pallas_call x1, Pallas kernels, local(): pl.pallas_call(kernel, out_shape=(out, out, out), in_specs=[pl.BlockSpec(...  53.9 us
    unnamed x7, local copies, waits for them, and re-layouts  2.77 us

profile of v2, /device:TPU:0, one launch (start us, length us, event | category | flops | bytes accessed | tf_op | source)
XLA Modules:
  0.0 57.3 jit_solution(4047534491304458643)
XLA Ops:
  0.6 53.9 %cg_step.1 = (f32[16,512]{1,0:T(8,128)}, f32[16,512]{1,0:T(8,128)}, f32[16,512]{1,0:T(8,128)}) custom-call(bf16[64,512]{1,0:T(8,128)(2,1)} %points_hbm.1, f32[1,64]{1,0:T(1,128)} %bitcast.3, f32[1,512]{1,0:T(1,128)} %bitcast.2, f32[16,512]{1,0:T(8,128)} %solution_hbm.1, f32[16,512]{1,0:T(8,128)} %residual_hbm.1, f32[16,512]{1,0:T(8,128)} %direction_hbm.1), custom_call_target="tpu_custom_call" | custom-call | tf_op jit(solution)/shard_map/cg_step/pallas_call | solution.py:266
  54.5 0.0 copy-start.1
  54.5 1.4 %copy.12 = f32[16,512]{1,0:T(8,128)} copy(f32[16,512]{1,0:T(8,128)} %get-tuple-element.6) | data formatting | bytes 65536
  55.9 0.0 copy-done.1
  55.9 0.0 copy-start
  55.9 0.6 %copy.13 = f32[16,512]{1,0:T(8,128)} copy(f32[16,512]{1,0:T(8,128)S(1)} %copy-done.1) | data formatting | bytes 65536
  56.5 0.2 copy-done
  56.7 0.6 %copy.14 = f32[16,512]{1,0:T(8,128)} copy(f32[16,512]{1,0:T(8,128)S(1)} %copy-done) | data formatting | bytes 65536
Async XLA Ops:
  54.5 1.4 %copy-start.1 = (f32[16,512]{1,0:T(8,128)S(1)}, f32[16,512]{1,0:T(8,128)}, u32[]{:S(2)}) copy-start(f32[16,512]{1,0:T(8,128)} %get-tuple-element.7) | copy-start | bytes 98308
  55.9 0.8 %copy-start = (f32[16,512]{1,0:T(8,128)S(1)}, f32[16,512]{1,0:T(8,128)}, u32[]{:S(2)}) copy-start(f32[16,512]{1,0:T(8,128)} %get-tuple-element.8) | copy-start | bytes 98308

commit v3 on v2

v3 whole, which is shorter than its diff:
```python
import functools

import jax
import jax.numpy as jnp
from jax import lax
from jax.experimental import pallas as pl
from jax.experimental.pallas import tpu as pltpu
from jax.sharding import PartitionSpec as P

MESH = pl.DeviceIdType.MESH
FEAT = 64
RHS = 16
DEEP = FEAT + 16
ROWS = DEEP + RHS
SIDE = 4
LATE = 11

ORDER = (
    (0, 0), (1, 0), (3, 0), (0, 1), (0, 3), (2, 0), (1, 1), (1, 3),
    (3, 1), (3, 3), (0, 2), (1, 2), (3, 2), (2, 1), (2, 3), (2, 2),
)
SLOT = {offset: n for n, offset in enumerate(ORDER)}
WAVES = (
    [((0, 0), step, step, None) for step in ((1, 0), (3, 0), (0, 1), (0, 3))],
    [
        ((1, 0), (0, 1), (1, 1), None), ((3, 0), (0, 1), (3, 1), None),
        ((1, 0), (0, 3), (1, 3), None), ((3, 0), (0, 3), (3, 3), None),
        ((1, 0), (1, 0), (2, 0), 0), ((3, 0), (3, 0), (2, 0), 1),
        ((0, 1), (0, 1), (0, 2), 0), ((0, 3), (0, 3), (0, 2), 1),
    ],
    [
        ((2, 0), (0, 1), (2, 1), None), ((2, 0), (0, 3), (2, 3), None),
        ((1, 1), (0, 1), (1, 2), 0), ((1, 3), (0, 3), (1, 2), 1),
        ((3, 1), (0, 1), (3, 2), 0), ((3, 3), (0, 3), (3, 2), 1),
    ],
    [((2, 1), (0, 1), (2, 2), 0), ((2, 3), (0, 3), (2, 2), 1)],
)


def bias_rows(scaled, flip):
    values = scaled.astype(jnp.float32)
    half = -0.5 * jnp.sum(values * values, axis=0, keepdims=True)
    high = half.astype(jnp.bfloat16).astype(jnp.float32)
    rest = half - high
    middle = rest.astype(jnp.bfloat16).astype(jnp.float32)
    low = rest - middle
    width = scaled.shape[1]
    index = lax.broadcasted_iota(jnp.int32, (16, width), 0)
    first = 3 if flip else 0
    ones = 0 if flip else 3
    rows = jnp.where(index == first, high, 0.0)
    rows = jnp.where(index == first + 1, middle, rows)
    rows = jnp.where(index == first + 2, low, rows)
    rows = jnp.where((index >= ones) & (index < ones + 3), 1.0, rows)
    return rows.astype(jnp.bfloat16)


def kernel(
    points_hbm, lengths_hbm, noise_hbm, residual_hbm, direction_hbm,
    image_ref, step_ref, growth_ref,
    points_ref, lengths_ref, noise_ref, residual_ref, direction_ref,
    blocks, line, weights, lefts, cross, tiles, total, parts, sums_line, sums_plane, own_sums, line_sums,
    in_sem, plane_send, plane_recv, pair_send, pair_recv, line_send, line_recv,
    part_send, part_recv, sl_send, sl_recv, sp_send, sp_recv,
):
    width = points_ref.shape[1]
    row, col = lax.axis_index("row"), lax.axis_index("col")
    core = lax.rem(row, 2)
    chip = row // 2
    y, z = chip // SIDE, lax.rem(chip, SIDE)

    def at(first, second, dcore, dx):
        dy = first * core + second * (1 - core)
        dz = first * (1 - core) + second * core
        ny, nz = lax.rem(y + dy, SIDE), lax.rem(z + dz, SIDE)
        return ((ny * SIDE + nz) * 2 + lax.rem(core + dcore, 2), lax.rem(col + dx, SIDE))

    plane = [at(a, b, 0, 0) for a, b in ORDER[1:]]
    others = [(q, c) for c in range(2) for q in range(SIDE)][1:]
    row_line = [at(0, 0, c, q) for q, c in others]
    sibling = at(0, 0, 1, 0)

    barrier = pltpu.get_barrier_semaphore()
    greeted = plane[:4] + [at(0, 0, 0, 1), at(0, 0, 0, 3), sibling]
    for device in greeted:
        pl.semaphore_signal(barrier, inc=1, device_id=device, device_id_type=MESH)

    pairs = (
        (points_hbm, points_ref), (lengths_hbm, lengths_ref), (direction_hbm, direction_ref),
        (noise_hbm, noise_ref), (residual_hbm, residual_ref),
    )
    loads = [pltpu.make_async_copy(src, dst, in_sem.at[n]) for n, (src, dst) in enumerate(pairs)]
    for copy in loads:
        copy.start()
    total[...] = jnp.zeros_like(total)
    cross[1] = jnp.full(cross.shape[1:], -1e4, jnp.float32)
    tiles[0] = jnp.zeros(tiles.shape[1:], jnp.bfloat16)
    for copy in loads[:3]:
        copy.wait()

    diagonal = lax.broadcasted_iota(jnp.int32, (FEAT, FEAT), 0) == lax.broadcasted_iota(
        jnp.int32, (FEAT, FEAT), 1
    )
    lengths = jnp.sum(jnp.where(diagonal, lengths_ref[...], 0.0), axis=1, keepdims=True)
    scaled = (points_ref[...].astype(jnp.float32) / lengths).astype(jnp.bfloat16)
    blocks[0, 0:FEAT, :] = scaled
    blocks[0, FEAT:DEEP, :] = bias_rows(scaled, False)
    blocks[0, DEEP:ROWS, :] = direction_ref[...].astype(jnp.bfloat16)

    pl.semaphore_wait(barrier, len(greeted))

    def remote(src, dst, send, recv, device):
        return pltpu.make_async_remote_copy(
            src_ref=src, dst_ref=dst, send_sem=send, recv_sem=recv, device_id=device, device_id_type=MESH
        )

    def plane_copy(src, step, dst, half):
        rows = pl.ds(0, ROWS) if half is None else pl.ds(half * (ROWS // 2), ROWS // 2)
        return remote(
            blocks.at[SLOT[src], rows], blocks.at[SLOT[dst], rows], plane_send.at[SLOT[dst], half or 0],
            plane_recv.at[SLOT[dst], half or 0], at(*step, 0, 0),
        )

    waves = [[plane_copy(*entry) for entry in wave] for wave in WAVES]

    def pair_copy(p):
        return remote(blocks.at[p], blocks.at[16 + p], pair_send.at[p], pair_recv.at[p], sibling)

    def next_wave(n):
        for copy in waves[n]:
            copy.wait_recv()
        if n + 1 < len(waves):
            for copy in waves[n + 1]:
                copy.start()
        for slot in sorted({SLOT[entry[2]] for entry in WAVES[n]}):
            pair_copy(slot).start()

    line_near = [
        remote(blocks.at[0, pl.ds(0, FEAT)], line.at[q - 1], line_send.at[n], line_recv.at[n], at(0, 0, 0, q))
        for n, q in enumerate((1, 3))
    ]
    line_far = [
        remote(
            line.at[q - 1, pl.ds(n * (FEAT // 2), FEAT // 2)], line.at[1, pl.ds(n * (FEAT // 2), FEAT // 2)],
            line_send.at[2 + n], line_recv.at[2 + n], at(0, 0, 0, q),
        )
        for n, q in enumerate((1, 3))
    ]
    pair_copy(0).start()
    for copy in line_near + waves[0]:
        copy.start()

    def transpose(block):
        lefts[block, :, 0:DEEP] = blocks[block, 0:DEEP, :].T

    def set_rows(q, part):
        weights[0:FEAT, q * width : (q + 1) * width] = part
        weights[FEAT:DEEP, q * width : (q + 1) * width] = bias_rows(part, True)

    def cross_stage(block, q, slot):
        cross[slot] = jnp.dot(
            lefts[block, :, 0:DEEP], weights[:, q * width : (q + 1) * width], preferred_element_type=jnp.float32
        )

    def exp_stage(slot):
        tiles[slot] = jnp.exp(cross[slot]).astype(jnp.bfloat16)

    def sum_stage(block, q, slot):
        columns = pl.ds(pl.multiple_of(q * width, width), width)
        total[:, columns] += jnp.dot(
            blocks[block, DEEP:ROWS, :], tiles[slot], preferred_element_type=jnp.float32
        )

    def run(chunks, before, middle=None):
        lagged = before + chunks
        for c, (block, q) in enumerate(chunks):
            sum_stage(*lagged[c], c % 2)
            exp_stage((c + 1) % 2)
            cross_stage(block, q, c % 2)
            if middle is not None and c == len(chunks) // 2 - 1:
                middle()
        return chunks[-2:]

    def loop(first, last, chunks_of, before, top=None, middle=None):
        def body(p, carry):
            if top is not None:
                top(p)
            own = chunks_of(p - 1)[-2:]
            lag = [
                (jnp.where(p == first, old[0], new[0]), jnp.where(p == first, old[1], new[1]))
                for old, new in zip(before, own)
            ]
            run(chunks_of(p), lag, None if middle is None else functools.partial(middle, p))
            return carry

        lax.fori_loop(first, last, body, 0)
        return chunks_of(last - 1)[-2:]

    def both(p, parts_):
        return [(block, q) for block in (p, 16 + p) for q in parts_]

    set_rows(0, scaled)
    transpose(0)
    pair_copy(0).wait_recv()
    transpose(16)
    lag = run([(0, 0), (16, 0)], [(0, 0), (0, 0)])
    for near, far in zip(line_near, line_far):
        near.wait_recv()
        far.start()
    set_rows(1, line[0])
    set_rows(3, line[2])
    lag = run([(0, 1), (16, 1), (0, 3), (16, 3)], lag)
    next_wave(0)
    transpose(1)

    def pair_arrives(p):
        pair_copy(p).wait_recv()
        transpose(16 + p)

    lag = loop(
        1, 5, lambda p: both(p, (0, 1, 3)), lag, pair_arrives, lambda p: transpose(jnp.minimum(p + 1, 4))
    )
    for copy in line_far:
        copy.wait_recv()
    set_rows(2, line[1])
    lag = loop(0, 5, lambda p: both(p, (2,)), lag)
    next_wave(1)
    transpose(5)

    def arrives(p):
        pl.when(p == 9)(functools.partial(next_wave, 2))
        pl.when(p == 13)(functools.partial(next_wave, 3))
        pair_arrives(p)

    lag = loop(5, 16, lambda p: both(p, (1, 2, 3)), lag, arrives, lambda p: transpose(jnp.minimum(p + 1, 15)))

    def late(n):
        return (16 * lax.rem(n, 2) + 16 - LATE + n // 2, 0)

    lag = run([late(0), late(1)], lag)
    part_copies = [
        remote(
            total.at[:, pl.ds(q * width, width)], parts.at[q - 1], part_send.at[q - 1], part_recv.at[q - 1],
            at(0, 0, 0, SIDE - q),
        )
        for q in (1, 3, 2)
    ]
    for copy in part_copies:
        copy.start()
    rounds = (2 * LATE - 4) // 6
    lag = loop(0, rounds, lambda m: [late(6 * m + 2 + c) for c in range(6)], lag)
    lag = run([late(2 * LATE - 2), late(2 * LATE - 1)], lag)
    sum_stage(*lag[0], 0)
    exp_stage(1)
    sum_stage(*lag[1], 1)
    for copy in loads[3:]:
        copy.wait()
    residual, direction = residual_ref[...], direction_ref[...]
    image = total[:, 0:width] + noise_ref[...] * direction
    for copy, q in zip(part_copies, (1, 3, 2)):
        copy.wait_recv()
        image = image + parts[q - 1]

    image_ref[...] = image
    lane = lax.broadcasted_iota(jnp.int32, (RHS, 128), 1)
    side = lax.broadcasted_iota(jnp.int32, (RHS, 128), 0)
    packed = jnp.zeros((RHS, 128), jnp.float32)
    for n, product in enumerate((residual * residual, direction * image, residual * image, image * image)):
        packed = jnp.where(lane == RHS * n + side, jnp.sum(product, axis=1, keepdims=True), packed)
    own_sums[...] = jnp.sum(packed, axis=0, keepdims=True)
    sl_copies = [
        remote(own_sums, sums_line.at[n], sl_send.at[n], sl_recv.at[n], row_line[n]) for n in range(len(row_line))
    ]
    for copy in sl_copies:
        copy.start()
    for copy in sl_copies:
        copy.wait_recv()
    line_sums[...] = own_sums[...] + jnp.sum(sums_line[...], axis=0)
    sp_copies = [
        remote(line_sums, sums_plane.at[n], sp_send.at[n], sp_recv.at[n], plane[n]) for n in range(len(plane))
    ]
    for copy in sp_copies:
        copy.start()
    for copy in sp_copies:
        copy.wait_recv()
    packed = line_sums[...] + jnp.sum(sums_plane[...], axis=0)

    norm_old, curvature, mixed, square = (
        jnp.sum(jnp.where(lane == RHS * n + side, packed, 0.0), axis=1, keepdims=True) for n in range(4)
    )
    step_size = norm_old / curvature
    norm_new = norm_old + step_size * (step_size * square - 2.0 * mixed)
    step_ref[...] = jnp.broadcast_to(step_size, step_ref.shape)
    growth_ref[...] = jnp.broadcast_to(norm_new / norm_old, growth_ref.shape)

    for copy in line_near + line_far + sum(waves, []) + part_copies + sl_copies + sp_copies:
        copy.wait_send()
    for p in range(16):
        pair_copy(p).wait_send()


def local(points, lengths, noise_var, solution, residual, direction):
    width = points.shape[1]
    out = jax.ShapeDtypeStruct((RHS, width), jnp.float32)
    vmem, dma = pltpu.VMEM, pltpu.SemaphoreType.DMA
    wide = vmem((RHS, width), jnp.float32)
    image, step_size, growth = pl.pallas_call(
        kernel,
        out_shape=(out, out, out),
        in_specs=[pl.BlockSpec(memory_space=pl.ANY)] * 5,
        out_specs=(pl.BlockSpec(memory_space=vmem),) * 3,
        scratch_shapes=[
            vmem((FEAT, width), jnp.bfloat16),
            vmem((1, FEAT), jnp.float32),
            vmem((1, width), jnp.float32),
            wide,
            wide,
            vmem((32, ROWS, width), jnp.bfloat16),
            vmem((SIDE - 1, FEAT, width), jnp.bfloat16),
            vmem((DEEP, SIDE * width), jnp.bfloat16),
            vmem((32, width, 128), jnp.bfloat16),
            vmem((2, width, width), jnp.float32),
            vmem((2, width, width), jnp.bfloat16),
            vmem((RHS, SIDE * width), jnp.float32),
            vmem((SIDE - 1, RHS, width), jnp.float32),
            vmem((7, 1, 128), jnp.float32),
            vmem((15, 1, 128), jnp.float32),
            vmem((1, 128), jnp.float32),
            vmem((1, 128), jnp.float32),
            dma((5,)), dma((16, 2)), dma((16, 2)), dma((16,)), dma((16,)), dma((4,)), dma((4,)),
            dma((3,)), dma((3,)), dma((7,)), dma((7,)), dma((15,)), dma((15,)),
        ],
        compiler_params=pltpu.CompilerParams(
            collective_id=0, has_side_effects=True, vmem_limit_bytes=63 << 20
        ),
        name="cg_step",
    )(points, lengths.reshape(1, FEAT), noise_var.reshape(1, width), residual, direction)
    new_residual = residual - step_size * image
    return solution + step_size * direction, new_residual, new_residual + growth * direction


def solution(mesh):
    wide = P(None, ("row", "col"))
    return jax.shard_map(
        local,
        mesh=mesh,
        in_specs=(wide, P(), P(("row", "col")), wide, wide, wide),
        out_specs=(wide, wide, wide),
        check_vma=False,
    )
```

time: 57.8 us -> 54.6 us (0.945)
  local copies, waits for them, and re-layouts: 2.77 us -> 0.01 us
  Pallas kernels: 53.9 us -> 52.2 us
  other arithmetic: 0 us -> 1.44 us
    unnamed x7 -> x6, local copies, waits for them, and re-layouts: 2.77 us -> 0.01 us
    pallas_call x1, Pallas kernels: 53.9 us -> 52.2 us  [local(): pl.pallas_call(kernel, out_shape=(out, out, out), in_specs=[pl.BlockSpec(...]
    add x0 -> x1, other arithmetic: none -> 1.44 us  [local(): new_residual + growth * direction]
where the time goes in v3:
time: 54.6 us; the launch traced here: 54.4 us
  Pallas kernels  52.2 us (96%)
  other arithmetic  1.44 us (3%)
  between operations  0.69 us (1%)
    pallas_call x1, Pallas kernels, local(): pl.pallas_call(kernel, out_shape=(out, out, out), in_specs=[pl.BlockSpec(...  52.2 us
    add x1, other arithmetic, local(): new_residual + growth * direction  1.44 us

profile of v3, /device:TPU:0, one launch (start us, length us, event | category | flops | bytes accessed | tf_op | source)
XLA Modules:
  0.0 54.4 jit_solution(11070766238541746321)
XLA Ops:
  0.6 0.0 copy-start
  0.6 0.0 copy-start.1
  0.7 0.0 copy-start.2
  0.7 52.2 %cg_step.1 = (f32[16,512]{1,0:T(8,128)}, f32[16,512]{1,0:T(8,128)}, f32[16,512]{1,0:T(8,128)}) custom-call(bf16[64,512]{1,0:T(8,128)(2,1)} %points_hbm.1, f32[1,64]{1,0:T(1,128)} %bitcast.3, f32[1,512]{1,0:T(1,128)} %bitcast.2, f32[16,512]{1,0:T(8,128)} %residual_hbm.1, f32[16,512]{1,0:T(8,128)} %direction_hbm.1), custom_call_target="tpu_custom_call" | custom-call | tf_op jit(solution)/shard_map/cg_step/pallas_call | solution.py:307
  52.9 0.0 copy-done
  52.9 0.0 copy-done.1
  52.9 0.0 copy-done.2
  52.9 1.4 %multiply_add_fusion = (f32[16,512]{1,0:T(8,128)}, f32[16,512]{1,0:T(8,128)}, f32[16,512]{1,0:T(8,128)}) fusion(f32[16,512]{1,0:T(8,128)} %get-tuple-element.8, f32[16,512]{1,0:T(8,128)S(1)} %copy-done.1, f32[16,512]{1,0:T(8,128)S(1)} %copy-done, f32[16,512]{1,0:T(8,128)} %get-tuple-element.6, f32[16,512]{1,0:T(8,128)} %get-tuple-element.7, ...), kind=kLoop, calls=%fused_computation | loop fusion | flops 49152 | bytes 294912 | tf_op jit(solution)/shard_map/add | solution.py:339
Async XLA Ops:
  0.6 52.3 %copy-start = (f32[16,512]{1,0:T(8,128)S(1)}, f32[16,512]{1,0:T(8,128)}, u32[]{:S(2)}) copy-start(f32[16,512]{1,0:T(8,128)} %residual_hbm.1) | copy-start | bytes 98308
  0.6 52.3 %copy-start.1 = (f32[16,512]{1,0:T(8,128)S(1)}, f32[16,512]{1,0:T(8,128)}, u32[]{:S(2)}) copy-start(f32[16,512]{1,0:T(8,128)} %direction_hbm.1) | copy-start | bytes 98308
  0.7 52.3 %copy-start.2 = (f32[16,512]{1,0:T(8,128)S(1)}, f32[16,512]{1,0:T(8,128)}, u32[]{:S(2)}) copy-start(f32[16,512]{1,0:T(8,128)} %param.9) | copy-start | bytes 98308

commit v4 on v3

--- a/solution.py
+++ b/solution.py
@@ -57,8 +57,8 @@
 
 def kernel(
     points_hbm, lengths_hbm, noise_hbm, residual_hbm, direction_hbm,
-    image_ref, step_ref, growth_ref,
-    points_ref, lengths_ref, noise_ref, residual_ref, direction_ref,
+    image_hbm, step_ref, growth_ref,
+    image_ref, points_ref, lengths_ref, noise_ref, residual_ref, direction_ref,
     blocks, line, weights, lefts, cross, tiles, total, parts, sums_line, sums_plane, own_sums, line_sums,
     in_sem, plane_send, plane_recv, pair_send, pair_recv, line_send, line_recv,
     part_send, part_recv, sl_send, sl_recv, sp_send, sp_recv,
@@ -181,20 +181,21 @@
                 middle()
         return chunks[-2:]
 
-    def loop(first, last, chunks_of, before, top=None, middle=None):
-        def body(p, carry):
+    def loop(first, last, step, chunks_of, before, top=None, middle=None):
+        def body(n, carry):
+            p = first + step * n
             if top is not None:
                 top(p)
-            own = chunks_of(p - 1)[-2:]
+            own = chunks_of(p - step)[-2:]
             lag = [
-                (jnp.where(p == first, old[0], new[0]), jnp.where(p == first, old[1], new[1]))
+                (jnp.where(n == 0, old[0], new[0]), jnp.where(n == 0, old[1], new[1]))
                 for old, new in zip(before, own)
             ]
             run(chunks_of(p), lag, None if middle is None else functools.partial(middle, p))
             return carry
 
-        lax.fori_loop(first, last, body, 0)
-        return chunks_of(last - 1)[-2:]
+        lax.fori_loop(0, (last - first) // step, body, 0)
+        return chunks_of(last - step)[-2:]
 
     def both(p, parts_):
         return [(block, q) for block in (p, 16 + p) for q in parts_]
@@ -212,27 +213,42 @@
     lag = run([(0, 1), (16, 1), (0, 3), (16, 3)], lag)
     next_wave(0)
     transpose(1)
+    transpose(2)
 
     def pair_arrives(p):
         pair_copy(p).wait_recv()
         transpose(16 + p)
 
+    def two_arrive(p):
+        pair_arrives(p)
+        pair_arrives(p + 1)
+
+    def two(p, parts_):
+        return both(p, parts_) + both(p + 1, parts_)
+
+    def two_follow(last, p):
+        transpose(jnp.minimum(p + 2, last))
+        transpose(jnp.minimum(p + 3, last))
+
     lag = loop(
-        1, 5, lambda p: both(p, (0, 1, 3)), lag, pair_arrives, lambda p: transpose(jnp.minimum(p + 1, 4))
+        1, 5, 2, lambda p: two(p, (0, 1, 3)), lag, two_arrive, functools.partial(two_follow, 4)
     )
     for copy in line_far:
         copy.wait_recv()
     set_rows(2, line[1])
-    lag = loop(0, 5, lambda p: both(p, (2,)), lag)
+    lag = run([chunk for p in range(5) for chunk in both(p, (2,))], lag)
     next_wave(1)
     transpose(5)
+    transpose(6)
 
     def arrives(p):
         pl.when(p == 9)(functools.partial(next_wave, 2))
         pl.when(p == 13)(functools.partial(next_wave, 3))
-        pair_arrives(p)
-
-    lag = loop(5, 16, lambda p: both(p, (1, 2, 3)), lag, arrives, lambda p: transpose(jnp.minimum(p + 1, 15)))
+        two_arrive(p)
+
+    lag = loop(5, 15, 2, lambda p: two(p, (1, 2, 3)), lag, arrives, functools.partial(two_follow, 15))
+    pair_arrives(15)
+    lag = run(both(15, (1, 2, 3)), lag)
 
     def late(n):
         return (16 * lax.rem(n, 2) + 16 - LATE + n // 2, 0)
@@ -248,7 +264,7 @@
     for copy in part_copies:
         copy.start()
     rounds = (2 * LATE - 4) // 6
-    lag = loop(0, rounds, lambda m: [late(6 * m + 2 + c) for c in range(6)], lag)
+    lag = loop(0, rounds, 1, lambda m: [late(6 * m + 2 + c) for c in range(6)], lag)
     lag = run([late(2 * LATE - 2), late(2 * LATE - 1)], lag)
     sum_stage(*lag[0], 0)
     exp_stage(1)
@@ -262,6 +278,8 @@
         image = image + parts[q - 1]
 
     image_ref[...] = image
+    image_out = pltpu.make_async_copy(image_ref, image_hbm, in_sem.at[0])
+    image_out.start()
     lane = lax.broadcasted_iota(jnp.int32, (RHS, 128), 1)
     side = lax.broadcasted_iota(jnp.int32, (RHS, 128), 0)
     packed = jnp.zeros((RHS, 128), jnp.float32)
@@ -273,6 +291,10 @@
     ]
     for copy in sl_copies:
         copy.start()
+    for copy in line_near + line_far + sum(waves, []) + part_copies:
+        copy.wait_send()
+    for p in range(16):
+        pair_copy(p).wait_send()
     for copy in sl_copies:
         copy.wait_recv()
     line_sums[...] = own_sums[...] + jnp.sum(sums_line[...], axis=0)
@@ -281,6 +303,9 @@
     ]
     for copy in sp_copies:
         copy.start()
+    for copy in sl_copies:
+        copy.wait_send()
+    image_out.wait()
     for copy in sp_copies:
         copy.wait_recv()
     packed = line_sums[...] + jnp.sum(sums_plane[...], axis=0)
@@ -293,10 +318,8 @@
     step_ref[...] = jnp.broadcast_to(step_size, step_ref.shape)
     growth_ref[...] = jnp.broadcast_to(norm_new / norm_old, growth_ref.shape)
 
-    for copy in line_near + line_far + sum(waves, []) + part_copies + sl_copies + sp_copies:
+    for copy in sp_copies:
         copy.wait_send()
-    for p in range(16):
-        pair_copy(p).wait_send()
 
 
 def local(points, lengths, noise_var, solution, residual, direction):
@@ -308,8 +331,9 @@
         kernel,
         out_shape=(out, out, out),
         in_specs=[pl.BlockSpec(memory_space=pl.ANY)] * 5,
-        out_specs=(pl.BlockSpec(memory_space=vmem),) * 3,
+        out_specs=(pl.BlockSpec(memory_space=pl.ANY),) + (pl.BlockSpec(memory_space=vmem),) * 2,
         scratch_shapes=[
+            wide,
             vmem((FEAT, width), jnp.bfloat16),
             vmem((1, FEAT), jnp.float32),
             vmem((1, width), jnp.float32),

time: 54.6 us -> 52.7 us (0.965)
  Pallas kernels: 52.2 us -> 50.3 us
    pallas_call x1, Pallas kernels: 52.2 us -> 50.3 us  [local(): pl.pallas_call(kernel, out_shape=(out, out, out), in_specs=[pl.BlockSpec(...]
where the time goes in v4:
time: 52.7 us; the launch traced here: 52.5 us
  Pallas kernels  50.3 us (95%)
  other arithmetic  1.44 us (3%)
  between operations  0.69 us (1%)
    pallas_call x1, Pallas kernels, local(): pl.pallas_call(kernel, out_shape=(out, out, out), in_specs=[pl.BlockSpec(...  50.3 us
    add x1, other arithmetic, local(): new_residual + growth * direction  1.44 us

profile of v4, /device:TPU:0, one launch (start us, length us, event | category | flops | bytes accessed | tf_op | source)
XLA Modules:
  0.0 52.5 jit_solution(7777754846626762871)
XLA Ops:
  0.6 0.0 copy-start
  0.6 0.0 copy-start.1
  0.7 0.0 copy-start.2
  0.7 50.3 %cg_step.1 = (f32[16,512]{1,0:T(8,128)}, f32[16,512]{1,0:T(8,128)}, f32[16,512]{1,0:T(8,128)}) custom-call(bf16[64,512]{1,0:T(8,128)(2,1)} %points_hbm.1, f32[1,64]{1,0:T(1,128)} %bitcast.3, f32[1,512]{1,0:T(1,128)} %bitcast.2, f32[16,512]{1,0:T(8,128)} %residual_hbm.1, f32[16,512]{1,0:T(8,128)} %direction_hbm.1), custom_call_target="tpu_custom_call" | custom-call | tf_op jit(solution)/shard_map/cg_step/pallas_call | solution.py:330
  51.0 0.0 copy-done
  51.0 0.0 copy-done.1
  51.0 0.0 copy-done.2
  51.0 1.4 %multiply_add_fusion = (f32[16,512]{1,0:T(8,128)}, f32[16,512]{1,0:T(8,128)}, f32[16,512]{1,0:T(8,128)}) fusion(f32[16,512]{1,0:T(8,128)} %get-tuple-element.8, f32[16,512]{1,0:T(8,128)S(1)} %copy-done.1, f32[16,512]{1,0:T(8,128)S(1)} %copy-done, f32[16,512]{1,0:T(8,128)} %get-tuple-element.6, f32[16,512]{1,0:T(8,128)} %get-tuple-element.7, ...), kind=kLoop, calls=%fused_computation | loop fusion | flops 49152 | bytes 294912 | tf_op jit(solution)/shard_map/add | solution.py:363
Async XLA Ops:
  0.6 50.4 %copy-start = (f32[16,512]{1,0:T(8,128)S(1)}, f32[16,512]{1,0:T(8,128)}, u32[]{:S(2)}) copy-start(f32[16,512]{1,0:T(8,128)} %residual_hbm.1) | copy-start | bytes 98308
  0.6 50.4 %copy-start.1 = (f32[16,512]{1,0:T(8,128)S(1)}, f32[16,512]{1,0:T(8,128)}, u32[]{:S(2)}) copy-start(f32[16,512]{1,0:T(8,128)} %direction_hbm.1) | copy-start | bytes 98308
  0.7 50.4 %copy-start.2 = (f32[16,512]{1,0:T(8,128)S(1)}, f32[16,512]{1,0:T(8,128)}, u32[]{:S(2)}) copy-start(f32[16,512]{1,0:T(8,128)} %param.9) | copy-start | bytes 98308

commit v5 on v4

--- a/solution.py
+++ b/solution.py
@@ -13,7 +13,7 @@
 DEEP = FEAT + 16
 ROWS = DEEP + RHS
 SIDE = 4
-LATE = 11
+LATE = 13
 
 ORDER = (
     (0, 0), (1, 0), (3, 0), (0, 1), (0, 3), (2, 0), (1, 1), (1, 3),
@@ -129,11 +129,11 @@
     def next_wave(n):
         for copy in waves[n]:
             copy.wait_recv()
+        for slot in sorted({SLOT[entry[2]] for entry in WAVES[n]}):
+            pair_copy(slot).start()
         if n + 1 < len(waves):
             for copy in waves[n + 1]:
                 copy.start()
-        for slot in sorted({SLOT[entry[2]] for entry in WAVES[n]}):
-            pair_copy(slot).start()
 
     line_near = [
         remote(blocks.at[0, pl.ds(0, FEAT)], line.at[q - 1], line_send.at[n], line_recv.at[n], at(0, 0, 0, q))
@@ -212,8 +212,8 @@
     set_rows(3, line[2])
     lag = run([(0, 1), (16, 1), (0, 3), (16, 3)], lag)
     next_wave(0)
-    transpose(1)
-    transpose(2)
+    for p in range(1, 5):
+        transpose(p)
 
     def pair_arrives(p):
         pair_copy(p).wait_recv()
@@ -230,16 +230,20 @@
         transpose(jnp.minimum(p + 2, last))
         transpose(jnp.minimum(p + 3, last))
 
-    lag = loop(
-        1, 5, 2, lambda p: two(p, (0, 1, 3)), lag, two_arrive, functools.partial(two_follow, 4)
-    )
+    early = [(p, q) for p in range(1, 5) for q in ((0, 1, 3) if p < 3 else (1, 3))]
+    lag = run(early, lag)
+    two_arrive(1)
+    two_arrive(3)
+    lag = run([(16 + p, q) for p, q in early], lag)
     for copy in line_far:
         copy.wait_recv()
     set_rows(2, line[1])
-    lag = run([chunk for p in range(5) for chunk in both(p, (2,))], lag)
+    far = [chunk for p in range(5) for chunk in both(p, (2,))]
+    lag = run(far[:4], lag)
     next_wave(1)
     transpose(5)
     transpose(6)
+    lag = run(far[4:], lag)
 
     def arrives(p):
         pl.when(p == 9)(functools.partial(next_wave, 2))
@@ -263,9 +267,7 @@
     ]
     for copy in part_copies:
         copy.start()
-    rounds = (2 * LATE - 4) // 6
-    lag = loop(0, rounds, 1, lambda m: [late(6 * m + 2 + c) for c in range(6)], lag)
-    lag = run([late(2 * LATE - 2), late(2 * LATE - 1)], lag)
+    lag = loop(0, (2 * LATE - 2) // 12, 1, lambda m: [late(12 * m + 2 + c) for c in range(12)], lag)
     sum_stage(*lag[0], 0)
     exp_stage(1)
     sum_stage(*lag[1], 1)

time: 52.7 us -> 50.9 us (0.966)
  Pallas kernels: 50.3 us -> 48.5 us
    pallas_call x1, Pallas kernels: 50.3 us -> 48.5 us  [local(): pl.pallas_call(kernel, out_shape=(out, out, out), in_specs=[pl.BlockSpec(...]
where the time goes in v5:
time: 50.9 us; the launch traced here: 50.7 us
  Pallas kernels  48.5 us (95%)
  other arithmetic  1.44 us (3%)
  between operations  0.69 us (1%)
    pallas_call x1, Pallas kernels, local(): pl.pallas_call(kernel, out_shape=(out, out, out), in_specs=[pl.BlockSpec(...  48.5 us
    add x1, other arithmetic, local(): new_residual + growth * direction  1.44 us

profile of v5, /device:TPU:0, one launch (start us, length us, event | category | flops | bytes accessed | tf_op | source)
XLA Modules:
  0.0 50.7 jit_solution(5764786428095115486)
XLA Ops:
  0.6 0.0 copy-start
  0.6 0.0 copy-start.1
  0.7 0.0 copy-start.2
  0.7 48.5 %cg_step.1 = (f32[16,512]{1,0:T(8,128)}, f32[16,512]{1,0:T(8,128)}, f32[16,512]{1,0:T(8,128)}) custom-call(bf16[64,512]{1,0:T(8,128)(2,1)} %points_hbm.1, f32[1,64]{1,0:T(1,128)} %bitcast.3, f32[1,512]{1,0:T(1,128)} %bitcast.2, f32[16,512]{1,0:T(8,128)} %residual_hbm.1, f32[16,512]{1,0:T(8,128)} %direction_hbm.1), custom_call_target="tpu_custom_call" | custom-call | tf_op jit(solution)/shard_map/cg_step/pallas_call | solution.py:332
  49.2 0.0 copy-done
  49.2 0.0 copy-done.1
  49.2 0.0 copy-done.2
  49.2 1.4 %multiply_add_fusion = (f32[16,512]{1,0:T(8,128)}, f32[16,512]{1,0:T(8,128)}, f32[16,512]{1,0:T(8,128)}) fusion(f32[16,512]{1,0:T(8,128)} %get-tuple-element.8, f32[16,512]{1,0:T(8,128)S(1)} %copy-done.1, f32[16,512]{1,0:T(8,128)S(1)} %copy-done, f32[16,512]{1,0:T(8,128)} %get-tuple-element.6, f32[16,512]{1,0:T(8,128)} %get-tuple-element.7, ...), kind=kLoop, calls=%fused_computation | loop fusion | flops 49152 | bytes 294912 | tf_op jit(solution)/shard_map/add | solution.py:365
Async XLA Ops:
  0.6 48.6 %copy-start = (f32[16,512]{1,0:T(8,128)S(1)}, f32[16,512]{1,0:T(8,128)}, u32[]{:S(2)}) copy-start(f32[16,512]{1,0:T(8,128)} %residual_hbm.1) | copy-start | bytes 98308
  0.6 48.6 %copy-start.1 = (f32[16,512]{1,0:T(8,128)S(1)}, f32[16,512]{1,0:T(8,128)}, u32[]{:S(2)}) copy-start(f32[16,512]{1,0:T(8,128)} %direction_hbm.1) | copy-start | bytes 98308
  0.7 48.6 %copy-start.2 = (f32[16,512]{1,0:T(8,128)S(1)}, f32[16,512]{1,0:T(8,128)}, u32[]{:S(2)}) copy-start(f32[16,512]{1,0:T(8,128)} %param.9) | copy-start | bytes 98308

commit v6 on v5

--- a/solution.py
+++ b/solution.py
@@ -239,18 +239,21 @@
         copy.wait_recv()
     set_rows(2, line[1])
     far = [chunk for p in range(5) for chunk in both(p, (2,))]
-    lag = run(far[:4], lag)
+    lag = run(far, lag)
     next_wave(1)
     transpose(5)
     transpose(6)
-    lag = run(far[4:], lag)
+    second = [(p, q) for p in (5, 6) for q in (1, 2, 3)]
+    lag = run(second, lag)
+    two_arrive(5)
+    lag = run([(16 + p, q) for p, q in second], lag, functools.partial(two_follow, 15, 5))
 
     def arrives(p):
         pl.when(p == 9)(functools.partial(next_wave, 2))
         pl.when(p == 13)(functools.partial(next_wave, 3))
         two_arrive(p)
 
-    lag = loop(5, 15, 2, lambda p: two(p, (1, 2, 3)), lag, arrives, functools.partial(two_follow, 15))
+    lag = loop(7, 15, 2, lambda p: two(p, (1, 2, 3)), lag, arrives, functools.partial(two_follow, 15))
     pair_arrives(15)
     lag = run(both(15, (1, 2, 3)), lag)
 

time: 50.9 us -> 50.8 us (level)
  no operation moved by 1% of the time
where the time goes in v6:
time: 50.8 us; the launch traced here: 50.6 us
  Pallas kernels  48.5 us (95%)
  other arithmetic  1.44 us (3%)
  between operations  0.69 us (1%)
    pallas_call x1, Pallas kernels, local(): pl.pallas_call(kernel, out_shape=(out, out, out), in_specs=[pl.BlockSpec(...  48.5 us
    add x1, other arithmetic, local(): new_residual + growth * direction  1.44 us

profile of v6, /device:TPU:0, one launch (start us, length us, event | category | flops | bytes accessed | tf_op | source)
XLA Modules:
  0.0 50.6 jit_solution(7858307724595713392)
XLA Ops:
  0.6 0.0 copy-start
  0.6 0.0 copy-start.1
  0.7 0.0 copy-start.2
  0.7 48.5 %cg_step.1 = (f32[16,512]{1,0:T(8,128)}, f32[16,512]{1,0:T(8,128)}, f32[16,512]{1,0:T(8,128)}) custom-call(bf16[64,512]{1,0:T(8,128)(2,1)} %points_hbm.1, f32[1,64]{1,0:T(1,128)} %bitcast.3, f32[1,512]{1,0:T(1,128)} %bitcast.2, f32[16,512]{1,0:T(8,128)} %residual_hbm.1, f32[16,512]{1,0:T(8,128)} %direction_hbm.1), custom_call_target="tpu_custom_call" | custom-call | tf_op jit(solution)/shard_map/cg_step/pallas_call | solution.py:335
  49.1 0.0 copy-done
  49.1 0.0 copy-done.1
  49.2 0.0 copy-done.2
  49.2 1.4 %multiply_add_fusion = (f32[16,512]{1,0:T(8,128)}, f32[16,512]{1,0:T(8,128)}, f32[16,512]{1,0:T(8,128)}) fusion(f32[16,512]{1,0:T(8,128)} %get-tuple-element.8, f32[16,512]{1,0:T(8,128)S(1)} %copy-done.1, f32[16,512]{1,0:T(8,128)S(1)} %copy-done, f32[16,512]{1,0:T(8,128)} %get-tuple-element.6, f32[16,512]{1,0:T(8,128)} %get-tuple-element.7, ...), kind=kLoop, calls=%fused_computation | loop fusion | flops 49152 | bytes 294912 | tf_op jit(solution)/shard_map/add | solution.py:368
Async XLA Ops:
  0.6 48.5 %copy-start = (f32[16,512]{1,0:T(8,128)S(1)}, f32[16,512]{1,0:T(8,128)}, u32[]{:S(2)}) copy-start(f32[16,512]{1,0:T(8,128)} %residual_hbm.1) | copy-start | bytes 98308
  0.6 48.5 %copy-start.1 = (f32[16,512]{1,0:T(8,128)S(1)}, f32[16,512]{1,0:T(8,128)}, u32[]{:S(2)}) copy-start(f32[16,512]{1,0:T(8,128)} %direction_hbm.1) | copy-start | bytes 98308
  0.7 48.5 %copy-start.2 = (f32[16,512]{1,0:T(8,128)S(1)}, f32[16,512]{1,0:T(8,128)}, u32[]{:S(2)}) copy-start(f32[16,512]{1,0:T(8,128)} %param.9) | copy-start | bytes 98308
